TPU v7x, 512 devices: a whole 4x8x8 slice. The times are simulated.
512 devices in a mesh: band: 32 (over x, z_lo, core), plane: 16 (over y, z_hi).
Axes of the slice: x: 4, y: 8, z: 8 (z_hi: 2, z_lo: 4; z = z_hi * 4 + z_lo), core: 2. Of those that a mesh axis runs over, the one named last changes fastest.
Arguments:
- orbitals: float32 [64, 128, 128, 128], P('band', 'plane'), may hold values from -6 to 6
- plan: int32 [2], replicated, may hold values from 0 to 63
- cutoff_mask: int32 [128, 128, 128], P(None, 'plane'), may hold values 0 or 1
Outputs:
- exchange_action: float32 [64, 128, 128, 128], P('band', 'plane')
All inputs are finite; a program needn't handle non-finite values. No bound on the sum of `cutoff_mask` on one device may be relied on, other than what follows from the above.
Results may differ from a plain program's by a relative error of at most 0.00027.
Values sent between devices are 32-bit elements; how exact they have to be, the bound alone decides.
A program may use at most 64 MiB of HBM per device.

v0:
```python
import math

import jax
import jax.numpy as jnp
from jax import lax
from jax.sharding import PartitionSpec as P


def broadcast(value, axis, source):
    kept = jnp.where(lax.axis_index(axis) == source, value, 0).astype(value.dtype)
    return lax.psum(kept, axis)


def cas_table(size):
    index = jnp.arange(size, dtype=jnp.int32)
    product = index[:, None] * index[None, :] % size
    angle = product.astype(jnp.float32) * (2.0 * math.pi / size)
    return jnp.cos(angle) + jnp.sin(angle)


def screened_kernel(size, offset, count):
    first = jnp.arange(size, dtype=jnp.int32)
    second = offset + jnp.arange(count, dtype=jnp.int32)
    signed_a = jnp.where(first < size // 2, first, first - size).astype(jnp.float32)
    signed_b = jnp.where(second < size // 2, second, second - size).astype(jnp.float32)
    wave_a = signed_a * (2.0 * math.pi / 41.04)
    wave_b = signed_b * (2.0 * math.pi / 41.04)
    wave_c = signed_a * (2.0 * math.pi / 20.52)
    squared = wave_a[:, None, None] ** 2 + wave_b[None, :, None] ** 2 + wave_c[None, None, :] ** 2
    omega = 0.106
    safe = jnp.where(squared > 0, squared, 1.0)
    screened = -4.0 * math.pi * (1.0 - jnp.exp(-safe / (4.0 * omega * omega))) / safe
    return jnp.where(squared > 0, screened, -math.pi / (omega * omega))


def along_last(field, table):
    return jnp.einsum("bxyz,kz->bxyk", field, table, precision=lax.Precision.HIGHEST)


def along_second(field, table):
    return jnp.einsum("bxyz,ky->bxkz", field, table, precision=lax.Precision.HIGHEST)


def along_first(field, table):
    return jnp.einsum("bxyz,kx->bkyz", field, table, precision=lax.Precision.HIGHEST)


def body(orbitals, plan, cutoff_mask):
    bands = orbitals.shape[0]
    size = orbitals.shape[2]
    steps = plan.shape[0]
    table = cas_table(size)
    columns = cutoff_mask.shape[1]
    offset = lax.axis_index("plane") * columns
    kernel = screened_kernel(size, offset, columns) * cutoff_mask.astype(jnp.float32)
    scale = 1.0 / (size * size * size)
    sources = []
    for step in range(steps):
        chosen = plan[step]
        local = lax.dynamic_index_in_dim(orbitals, chosen % bands, 0, keepdims=False)
        sources.append(broadcast(local, "band", chosen // bands))

    def filter_split(block):
        spectrum = along_first(block, table)
        back = along_first(kernel[None] * spectrum, table)
        return lax.all_to_all(back, "plane", split_axis=1, concat_axis=2, tiled=True)

    nearby = [along_second(along_last(orbitals * phi[None], table), table) for phi in sources]
    returned = [
        filter_split(lax.all_to_all(near, "plane", split_axis=2, concat_axis=1, tiled=True))
        for near in nearby
    ]
    total = jnp.zeros(orbitals.shape, jnp.float32)
    for step in range(steps):
        back = along_last(along_second(returned[step], table), table) * scale
        total = total + sources[step][None] * back
    return total


def solution(mesh):
    return jax.shard_map(
        body,
        mesh=mesh,
        in_specs=(P("band", "plane", None, None), P(), P(None, "plane", None)),
        out_specs=P("band", "plane", None, None),
        check_vma=False,
    )
```

profile of v0, /device:TPU:6, one launch (start us, length us, event | category | flops | bytes accessed | tf_op | source)
XLA Modules:
  0.0 488.8 jit_solution(16319307705160877634)
XLA Ops:
  12.7 2.3 select_bitcast_fusion
  15.0 276.5 %all-reduce.3.cloned.1.call-done = (f32[8,128,128]{2,1,0:T(8,128)}, f32[8,128,128]{2,1,0:T(8,128)}) async-done(((f32[8,128,128]{2,1,0:T(8,128)}, f32[8,128,128]{2,1,0:T(8,128)}), (f32[8,128,128]{2,1,0:T(8,128)}, f32[8,128,128]{2,1,0:T(8,128)})) %all-reduce.3.cloned.1.call-update) | async-done | bytes 1048592 | tf_op jit(solution)/shard_map/psum | solution.py:11
  291.5 2.3 fusion.11
  293.8 1.3 convolution_bitcast_fusion.5
  295.1 1.6 copy.18
  296.6 9.5 %all-to-all-start = ((f32[2,8,128,128]{3,1,0,2:T(8,128)}), f32[2,8,128,128]{3,1,0,2:T(8,128)S(1)}, u32[]{:S(2)}, u32[]{:S(2)}) async-start(f32[2,8,128,128]{3,1,0,2:T(8,128)} %copy.18), calls=%async_computation | async-start | bytes 2097152 | tf_op jit(solution)/shard_map/all_to_all | solution.py:70
  307.4 1.3 convolution_bitcast_fusion.2
  308.7 1.6 copy.25
  310.3 28.1 %all-to-all-done = f32[2,8,128,128]{3,1,0,2:T(8,128)S(1)} async-done(((f32[2,8,128,128]{3,1,0,2:T(8,128)}), f32[2,8,128,128]{3,1,0,2:T(8,128)S(1)}, u32[]{:S(2)}, u32[]{:S(2)}) %all-to-all-start) | async-done | bytes 1048608 | tf_op jit(solution)/shard_map/all_to_all | solution.py:70
  338.4 10.1 %all-to-all-start.2 = ((f32[2,8,128,128]{3,1,0,2:T(8,128)}), f32[2,8,128,128]{3,1,0,2:T(8,128)S(1)}, u32[]{:S(2)}, u32[]{:S(2)}) async-start(f32[2,8,128,128]{3,1,0,2:T(8,128)} %copy.25), calls=%async_computation.2 | async-start | bytes 2097152 | tf_op jit(solution)/shard_map/all_to_all | solution.py:70
  349.4 1.3 fusion.2
  350.8 1.3 convolution_bitcast_fusion.4
  352.1 1.6 copy.22
  353.7 34.3 %all-to-all-done.2 = f32[2,8,128,128]{3,1,0,2:T(8,128)S(1)} async-done(((f32[2,8,128,128]{3,1,0,2:T(8,128)}), f32[2,8,128,128]{3,1,0,2:T(8,128)S(1)}, u32[]{:S(2)}, u32[]{:S(2)}) %all-to-all-start.2) | async-done | bytes 1048608 | tf_op jit(solution)/shard_map/all_to_all | solution.py:70
  387.9 7.8 %all-to-all-start.1 = ((f32[2,128,8,128]{3,2,0,1:T(8,128)}), f32[2,128,8,128]{3,2,0,1:T(8,128)S(1)}, u32[]{:S(2)}, u32[]{:S(2)}) async-start(f32[2,128,8,128]{3,2,0,1:T(8,128)} %copy.22), calls=%async_computation.1 | async-start | bytes 2097152 | tf_op jit(solution)/shard_map/all_to_all | solution.py:66
  396.1 1.3 fusion.1
  397.4 1.3 convolution_bitcast_fusion.1
  398.7 1.6 copy.29
  400.3 33.6 %all-to-all-done.1 = f32[2,128,8,128]{3,2,0,1:T(8,128)S(1)} async-done(((f32[2,128,8,128]{3,2,0,1:T(8,128)}), f32[2,128,8,128]{3,2,0,1:T(8,128)S(1)}, u32[]{:S(2)}, u32[]{:S(2)}) %all-to-all-start.1) | async-done | bytes 1048608 | tf_op jit(solution)/shard_map/all_to_all | solution.py:66
  433.9 8.2 %all-to-all-start.3 = ((f32[2,128,8,128]{3,2,0,1:T(8,128)}), f32[2,128,8,128]{3,2,0,1:T(8,128)S(1)}, u32[]{:S(2)}, u32[]{:S(2)}) async-start(f32[2,128,8,128]{3,2,0,1:T(8,128)} %copy.29), calls=%async_computation.3 | async-start | bytes 2097152 | tf_op jit(solution)/shard_map/all_to_all | solution.py:66
  443.2 1.3 convolution_bitcast_fusion.3
  444.5 32.7 %all-to-all-done.3 = f32[2,128,8,128]{3,2,0,1:T(8,128)S(1)} async-done(((f32[2,128,8,128]{3,2,0,1:T(8,128)}), f32[2,128,8,128]{3,2,0,1:T(8,128)S(1)}, u32[]{:S(2)}, u32[]{:S(2)}) %all-to-all-start.3) | async-done | bytes 1048608 | tf_op jit(solution)/shard_map/all_to_all | solution.py:66
  477.1 1.3 convolution_bitcast_fusion
  479.7 2.2 fusion
  (28 shorter events, 6.0 us)
Async XLA Ops:
  6.5 0.7 copy-start.6
  6.5 284.9 %all-reduce.3.cloned.1.call-start = ((), (), s32[]{:S(2)}) async-start(), calls=%async_computation.4 | async-start | bytes 2097152 | tf_op jit(solution)/shard_map/psum | solution.py:11
  14.9 276.5 %copy-start = (f32[2,8,128,128]{3,2,1,0:T(8,128)S(1)}, f32[2,8,128,128]{3,2,1,0:T(8,128)}, u32[]{:S(2)}) copy-start(f32[2,8,128,128]{3,2,1,0:T(8,128)} %param.3) | copy-start | bytes 3145732
  296.6 9.5 %copy-start.2 = (f32[8,128,128]{2,1,0:T(8,128)S(1)}, f32[8,128,128]{2,1,0:T(8,128)}, u32[]{:S(2)}) copy-start(f32[8,128,128]{2,1,0:T(8,128)} %get-tuple-element.6) | copy-start | bytes 1572868
  296.6 41.8 %all-to-all-start = ((f32[2,8,128,128]{3,1,0,2:T(8,128)}), f32[2,8,128,128]{3,1,0,2:T(8,128)S(1)}, u32[]{:S(2)}, u32[]{:S(2)}) async-start(f32[2,8,128,128]{3,1,0,2:T(8,128)} %copy.18), calls=%async_computation | async-start | bytes 2097152 | tf_op jit(solution)/shard_map/all_to_all | solution.py:70
  310.3 38.4 %copy-start.5 = (s32[128,8,128]{2,1,0:T(8,128)S(1)}, s32[128,8,128]{2,1,0:T(8,128)}, u32[]{:S(2)}) copy-start(s32[128,8,128]{2,1,0:T(8,128)} %param.5) | copy-start | bytes 1572868
  338.4 49.5 %all-to-all-start.2 = ((f32[2,8,128,128]{3,1,0,2:T(8,128)}), f32[2,8,128,128]{3,1,0,2:T(8,128)S(1)}, u32[]{:S(2)}, u32[]{:S(2)}) async-start(f32[2,8,128,128]{3,1,0,2:T(8,128)} %copy.25), calls=%async_computation.2 | async-start | bytes 2097152 | tf_op jit(solution)/shard_map/all_to_all | solution.py:70
  387.9 46.0 %all-to-all-start.1 = ((f32[2,128,8,128]{3,2,0,1:T(8,128)}), f32[2,128,8,128]{3,2,0,1:T(8,128)S(1)}, u32[]{:S(2)}, u32[]{:S(2)}) async-start(f32[2,128,8,128]{3,2,0,1:T(8,128)} %copy.22), calls=%async_computation.1 | async-start | bytes 2097152 | tf_op jit(solution)/shard_map/all_to_all | solution.py:66
  400.3 41.8 %copy-start.1 = (f32[8,128,128]{2,1,0:T(8,128)S(1)}, f32[8,128,128]{2,1,0:T(8,128)}, u32[]{:S(2)}) copy-start(f32[8,128,128]{2,1,0:T(8,128)} %get-tuple-element.5) | copy-start | bytes 1572868
  433.9 43.2 %all-to-all-start.3 = ((f32[2,128,8,128]{3,2,0,1:T(8,128)}), f32[2,128,8,128]{3,2,0,1:T(8,128)S(1)}, u32[]{:S(2)}, u32[]{:S(2)}) async-start(f32[2,128,8,128]{3,2,0,1:T(8,128)} %copy.29), calls=%async_computation.3 | async-start | bytes 2097152 | tf_op jit(solution)/shard_map/all_to_all | solution.py:66
  477.1 1.3 copy-start.4
  478.4 1.3 copy-start.3
Sparse Core Ops, SparseCore 0:
  15.1 276.3 all-reduce.2
where the time goes:
time: 489 us
  waiting for transfers between devices  405 us (83%)
  starting transfers between devices  35.6 us (7%)
  between operations  18.5 us (4%)
  matrix products  17.4 us (4%)
  local copies, waits for them, and re-layouts  8.41 us (2%)
    psum x1, waiting for transfers between devices, broadcast(): return lax.psum(kept, axis)  277 us
    all_to_all x2, waiting for transfers between devices, filter_split(): lax.all_to_all(back, 'plane', split_axis=1, concat_axis=2, tiled=True)  66.3 us
    all_to_all x2, waiting for transfers between devices, body(): lax.all_to_all(near, 'plane', split_axis=2, concat_axis=1, tiled=True)  62.4 us
    all_to_all x2, starting transfers between devices, body(): lax.all_to_all(near, 'plane', split_axis=2, concat_axis=1, tiled=True)  19.6 us
    all_to_all x2, starting transfers between devices, filter_split(): lax.all_to_all(back, 'plane', split_axis=1, concat_axis=2, tiled=True)  16 us
  transfers between devices with their start and end apart: 5, of which 5 were waited for; matrix products, arithmetic and copies ran while one was open for 3% of the time, Pallas kernels for 0%

commit v1 on v0

v1 whole, which is shorter than its diff:
```python
import functools
import math

import jax
import jax.numpy as jnp
import numpy as np
from jax import lax
from jax.experimental import pallas as pl
from jax.experimental.pallas import tpu as pltpu
from jax.sharding import PartitionSpec as P

MESH = pl.DeviceIdType.MESH
F32 = jnp.float32
BF16 = jnp.bfloat16
OMEGA = 0.106


def cas_table(size):
    index = np.arange(size, dtype=np.int64)
    angle = (index[:, None] * index[None, :] % size) * (2.0 * math.pi / size)
    return (np.cos(angle) + np.sin(angle)).astype(np.float32)


def split(value):
    high = value.astype(BF16)
    low = (value - high.astype(F32)).astype(BF16)
    return high, low


def product(left, right):
    a = jnp.concatenate([left[0], left[1], left[0]], axis=1)
    b = jnp.concatenate([right[0], right[0], right[1]], axis=0)
    return jnp.dot(a, b, preferred_element_type=F32)


def kernel(
    bands, planes, steps, size, slab,
    plan_ref, orb_ref, mask_ref, table_ref, out_ref,
    filt, cand, mixed, crossed, scattered, phi, sent, landed, filtered, returned,
    core_send, core_recv, scat_send, scat_recv, gath_send, gath_recv, half_send, half_recv,
    fwd_send, fwd_recv, back_send, back_recv,
):
    band = lax.axis_index("band")
    plane = lax.axis_index("plane")
    core = lax.rem(band, 2)
    chip = band // 2
    chips = bands // 2
    rings = planes // 2
    y = plane // 2
    zh = lax.rem(plane, 2)
    half = slab // 2 * size
    piece = half // chips

    order = []
    for far in sorted(range(1, rings), key=lambda d: -min(d, rings - d)):
        order += [(far, 1), (far, 0)]
    order.append((0, 1))

    def partner(far, other):
        return lax.rem(y + far, rings) * 2 + lax.rem(zh + other, 2)

    others = [(lax.rem(chip + k, chips) * 2 + core, plane) for k in range(1, chips)]
    twin = (chip * 2 + 1 - core, plane)

    barrier = pltpu.get_barrier_semaphore()
    greeted = [twin] + others + [(band, partner(*o)) for o in order]
    for device in greeted:
        pl.semaphore_signal(barrier, inc=1, device_id=device, device_id_type=MESH)

    row = lax.broadcasted_iota(jnp.int32, (size, size), 0)
    col = lax.broadcasted_iota(jnp.int32, (size, size), 1)

    def wave(index, cell):
        return jnp.where(index < size // 2, index, index - size).astype(F32) * (2.0 * math.pi / cell)

    wave_ac = wave(row, 41.04) ** 2 + wave(col, 20.52) ** 2

    def screen(k, _):
        second = plane * slab + k
        wave_b = wave(jnp.full((size, size), second, jnp.int32), 41.04)
        squared = wave_ac + wave_b * wave_b
        safe = jnp.where(squared > 0, squared, 1.0)
        screened = -4.0 * math.pi * (1.0 - jnp.exp(-safe / (4.0 * OMEGA * OMEGA))) / safe
        screened = jnp.where(squared > 0, screened, -math.pi / (OMEGA * OMEGA))
        keep = mask_ref[pl.ds(k, size, stride=slab), :].astype(F32)
        filt[k] = screened * keep * (1.0 / (size * size * size))
        return _

    lax.fori_loop(0, slab, screen, 0)
    for s in range(steps):
        first = (plan_ref[s] == 2 * band).astype(F32)
        second = (plan_ref[s] == 2 * band + 1).astype(F32)
        cand[s] = orb_ref[0] * first + orb_ref[1] * second

    pl.semaphore_wait(barrier, len(greeted))

    def copy(src, dst, send, recv, device):
        return pltpu.make_async_remote_copy(
            src_ref=src, dst_ref=dst, send_sem=send, recv_sem=recv, device_id=device, device_id_type=MESH
        )

    mine = pl.ds(pl.multiple_of(core * half, half), half)
    theirs = pl.ds(pl.multiple_of((1 - core) * half, half), half)

    def core_copy(s):
        return copy(cand.at[s, theirs], crossed.at[s], core_send.at[s], core_recv.at[s], twin)

    def chunk(k):
        return pl.ds(pl.multiple_of(k * piece, piece), piece)

    def scatter_copy(s, k):
        target = lax.rem(chip + k, chips)
        return copy(
            mixed.at[s, chunk(target)], scattered.at[s, chip], scat_send.at[s, k], scat_recv.at[s, k], others[k - 1]
        )

    def gather_copy(s, k):
        where = pl.ds(pl.multiple_of(core * half + chip * piece, piece), piece)
        return copy(phi.at[s, where], phi.at[s, where], gath_send.at[s, k], gath_recv.at[s, k], others[k - 1])

    def half_copy(s):
        return copy(phi.at[s, mine], phi.at[s, mine], half_send.at[s], half_recv.at[s], twin)

    def scatter(s):
        core_copy(s).wait_recv()
        mixed[s] = cand[s, mine] + crossed[s]
        for k in range(1, chips):
            scatter_copy(s, k).start()
        scattered[s, chip] = mixed[s, chunk(chip)]

    def gather(s):
        for k in range(1, chips):
            scatter_copy(s, k).wait_recv()
        total = scattered[s, 0]
        for k in range(1, chips):
            total = total + scattered[s, k]
        phi[s, pl.ds(pl.multiple_of(core * half + chip * piece, piece), piece)] = total
        for k in range(1, chips):
            gather_copy(s, k).start()

    def exchange(s):
        for k in range(1, chips):
            gather_copy(s, k).wait_recv()
        half_copy(s).start()

    table = split(table_ref[...])

    def forward_copy(s, b, k):
        q = partner(*order[k])
        return copy(
            sent.at[s, b, :, pl.ds(pl.multiple_of(q * slab, slab), slab)],
            landed.at[s, b, pl.ds(pl.multiple_of(plane * slab, slab), slab)],
            fwd_send.at[s, b, k], fwd_recv.at[s, b, k], (band, q),
        )

    def backward_copy(s, b, k):
        q = partner(*order[k])
        return copy(
            filtered.at[s, b, pl.ds(pl.multiple_of(q * slab, slab), slab)],
            returned.at[s, b, :, pl.ds(pl.multiple_of(plane * slab, slab), slab)],
            back_send.at[s, b, k], back_recv.at[s, b, k], (band, q),
        )

    own = pl.ds(pl.multiple_of(plane * slab, slab), slab)

    def pair(s, b):
        def one(x, _):
            rows = pl.ds(pl.multiple_of(x * size, size), size)
            field = orb_ref[b, rows] * phi[s, rows]
            field = product(split(field), table)
            sent[s, b, x] = product(table, split(field))
            return _

        lax.fori_loop(0, slab, one, 0)
        for k in range(len(order)):
            forward_copy(s, b, k).start()
        landed[s, b, own] = sent[s, b, :, own]

    def middle(s, b):
        for k in range(len(order)):
            forward_copy(s, b, k).wait_recv()
        source = landed.at[s, b].reshape(size * slab, size)
        target = filtered.at[s, b].reshape(size * slab, size)

        def one(k, _):
            field = source[pl.ds(k, size, stride=slab), :]
            field = product(table, split(field)) * filt[k]
            target[pl.ds(k, size, stride=slab), :] = product(table, split(field))
            return _

        lax.fori_loop(0, slab, one, 0)
        for k in range(len(order)):
            backward_copy(s, b, k).start()
        returned[s, b, :, own] = filtered[s, b, own]

    def last(s, b):
        for k in range(len(order)):
            backward_copy(s, b, k).wait_recv()

        def one(x, _):
            rows = pl.ds(pl.multiple_of(x * size, size), size)
            field = product(table, split(returned[s, b, x]))
            field = product(split(field), table) * phi[s, rows]
            if s == 0:
                out_ref[b, rows] = field
            else:
                out_ref[b, rows] += field
            return _

        lax.fori_loop(0, slab, one, 0)

    units = [(s, b) for s in range(steps) for b in range(2)]
    for s in range(steps):
        core_copy(s).start()
    for s in range(steps):
        scatter(s)
    for s in range(steps):
        gather(s)
    exchange(0)
    for s in range(steps):
        half_copy(s).wait_recv()
        pair(s, 0)
        if s + 1 < steps:
            exchange(s + 1)
        pair(s, 1)
    for unit in units:
        middle(*unit)
    for unit in units:
        last(*unit)

    for s in range(steps):
        core_copy(s).wait_send()
        half_copy(s).wait_send()
        for k in range(1, chips):
            scatter_copy(s, k).wait_send()
            gather_copy(s, k).wait_send()
    for s, b in units:
        for k in range(len(order)):
            forward_copy(s, b, k).wait_send()
            backward_copy(s, b, k).wait_send()


def body(bands, planes, orbitals, plan, cutoff_mask):
    own, slab, size = orbitals.shape[:3]
    steps = plan.shape[0]
    chips = bands // 2
    half = slab // 2 * size
    partners = planes - 1
    vmem = pl.BlockSpec(memory_space=pltpu.VMEM)
    dma = pltpu.SemaphoreType.DMA
    unit = (steps, own)
    out = pl.pallas_call(
        functools.partial(kernel, bands, planes, steps, size, slab),
        out_shape=jax.ShapeDtypeStruct((own, slab * size, size), F32),
        in_specs=[pl.BlockSpec(memory_space=pltpu.SMEM), vmem, vmem, vmem],
        out_specs=vmem,
        scratch_shapes=[
            pltpu.VMEM((slab, size, size), F32),
            pltpu.VMEM((steps, 2 * half, size), F32),
            pltpu.VMEM((steps, half, size), F32),
            pltpu.VMEM((steps, half, size), F32),
            pltpu.VMEM((steps, chips, half // chips, size), F32),
            pltpu.VMEM((steps, 2 * half, size), F32),
            pltpu.VMEM(unit + (slab, size, size), F32),
            pltpu.VMEM(unit + (size, slab, size), F32),
            pltpu.VMEM(unit + (size, slab, size), F32),
            pltpu.VMEM(unit + (slab, size, size), F32),
            dma((steps,)), dma((steps,)),
            dma((steps, chips)), dma((steps, chips)),
            dma((steps, chips)), dma((steps, chips)),
            dma((steps,)), dma((steps,)),
            dma(unit + (partners,)), dma(unit + (partners,)),
            dma(unit + (partners,)), dma(unit + (partners,)),
        ],
        compiler_params=pltpu.CompilerParams(
            collective_id=0, has_side_effects=True, vmem_limit_bytes=40 * 2**20
        ),
    )(
        plan,
        orbitals.reshape(own, slab * size, size),
        cutoff_mask.reshape(size * slab, size),
        jnp.asarray(cas_table(size)),
    )
    return out.reshape(orbitals.shape)


def solution(mesh):
    bands, planes = mesh.shape["band"], mesh.shape["plane"]
    return jax.shard_map(
        functools.partial(body, bands, planes),
        mesh=mesh,
        in_specs=(P("band", "plane", None, None), P(), P(None, "plane", None)),
        out_specs=P("band", "plane", None, None),
        check_vma=False,
    )
```

time: 489 us -> 157 us (0.32)
  the two profiles are of different devices: /device:TPU:6 before, /device:TPU:200 now
where the time goes in v1:
time: 157 us
  Pallas kernels  152 us (97%)
  local copies, waits for them, and re-layouts  4.73 us (3%)
    pallas_call x1, Pallas kernels, body(): pl.pallas_call(functools.partial(kernel, bands, planes, steps, size, slab...  152 us
    unnamed x9, local copies, waits for them, and re-layouts  4.73 us

profile of v1, /device:TPU:200, one launch (start us, length us, event | category | flops | bytes accessed | tf_op | source)
XLA Modules:
  0.0 156.6 jit_solution(11587203893099064046)
XLA Ops:
  0.0 0.0 copy-start.3
  0.0 0.7 copy-done.3
  0.7 0.0 copy-start
  0.7 1.2 copy-done
  1.9 0.0 copy-start.1
  1.9 1.0 copy-done.1
  2.9 0.0 copy-start.2
  2.9 0.8 copy-done.2
  3.8 151.8 %shard_map.46 = f32[2,1024,128]{2,1,0:T(8,128)S(1)} custom-call(s32[2]{0:T(128)S(1)} %copy-done.3, f32[2,1024,128]{2,1,0:T(8,128)S(1)} %bitcast.4, s32[1024,128]{1,0:T(8,128)S(1)} %bitcast.5, f32[128,128]{1,0:T(8,128)S(1)} %copy-done.2), custom_call_target="tpu_custom_call" | custom-call | tf_op jit(solution)/shard_map/pallas_call | solution.py:252
  155.6 1.0 copy.6
Async XLA Ops:
  0.0 0.7 copy-start.3
  0.7 1.2 copy-start
  1.9 1.0 copy-start.1
  2.9 0.8 copy-start.2

commit v2 on v0

v2 whole, which is shorter than its diff:
```python
import functools
import math

import jax
import jax.numpy as jnp
import numpy as np
from jax import lax
from jax.experimental import pallas as pl
from jax.experimental.pallas import tpu as pltpu
from jax.sharding import PartitionSpec as P

MESH = pl.DeviceIdType.MESH
F32 = jnp.float32
BF16 = jnp.bfloat16
OMEGA = 0.106
CORES, Z_LO, RING_X = 2, 4, 4


def cas_table(size):
    index = np.arange(size, dtype=np.int64)
    angle = (index[:, None] * index[None, :] % size) * (2.0 * math.pi / size)
    return (np.cos(angle) + np.sin(angle)).astype(np.float32)


def split(value):
    high = value.astype(BF16)
    low = (value - high.astype(F32)).astype(BF16)
    return high, low


def kernel(
    planes, steps, bands, size, slab, phi_parts, pair_parts,
    plan_hbm, orb_hbm, mask_hbm, table_hbm, out_ref,
    plan_ref, orb_ref, mask_ref, table_ref, filt, cand, crossed, mixed, spread, reduced, summed, phi,
    sent, landed, filtered, returned,
    calm, in_sem, core_send, core_recv, spread_send, spread_recv, z_send, z_recv, up_send, up_recv, gath_send, gath_recv,
    half_send, half_recv,
    fwd_send, fwd_recv, back_send, back_recv,
):
    band = lax.axis_index("band")
    plane = lax.axis_index("plane")
    core = lax.rem(band, CORES)
    z_lo = lax.rem(band // CORES, Z_LO)
    x = band // (CORES * Z_LO)
    rings = planes // 2
    y = plane // 2
    z_hi = lax.rem(plane, 2)
    here = x * CORES + core

    def device(e, z):
        return (e // CORES) * (CORES * Z_LO) + z * CORES + lax.rem(e, CORES)

    order = [(4, 1), (4, 0), (0, 1), (1, 1), (3, 0), (5, 0), (7, 1), (2, 1), (6, 1), (2, 0), (6, 0), (3, 1), (5, 1), (1, 0), (7, 0)]
    partners = [lax.rem(y + far, rings) * 2 + lax.rem(z_hi + other, 2) for far, other in order]
    levels = [lax.rem(z_lo + k, Z_LO) for k in range(1, Z_LO)]

    barrier = pltpu.get_barrier_semaphore()
    greeted = [(device(lax.rem(x + k, RING_X) * CORES + core, z_lo), plane) for k in range(1, RING_X)]
    greeted += [(device(x * CORES + 1 - core, z_lo), plane)]
    greeted += [(device(here, z), plane) for z in levels]
    greeted += [(band, q) for q in partners]
    column = [
        (device(x * CORES + lax.rem(core + k % CORES, CORES), lax.rem(z_lo + k // CORES % Z_LO, Z_LO)),
         2 * y + lax.rem(z_hi + k // (CORES * Z_LO), 2))
        for k in range(1, 2 * CORES * Z_LO)
    ]
    greeted += [column[k - 1] for k in range(1, 2 * CORES * Z_LO) if k % CORES and k != 1 or k > CORES * Z_LO and k % CORES == 0]
    for target in greeted:
        pl.semaphore_signal(barrier, inc=1, device_id=target, device_id_type=MESH)

    loads = [
        pltpu.make_async_copy(source, target, in_sem.at[i])
        for i, (source, target) in enumerate(
            ((plan_hbm, plan_ref), (orb_hbm, orb_ref), (table_hbm, table_ref), (mask_hbm, mask_ref))
        )
    ]
    for load in loads:
        load.start()
    loads[0].wait()
    loads[1].wait()
    for s in range(steps):
        first = (plan_ref[s] == 2 * band).astype(F32)
        second = (plan_ref[s] == 2 * band + 1).astype(F32)
        chosen = orb_ref[0] * first + orb_ref[1] * second
        cand[s] = chosen.reshape(cand.shape[1:])
    loads[2].wait()
    high, low = split(table_ref[...])
    table_left = jnp.concatenate([high, high, low], axis=1)
    table_right = jnp.concatenate([high, high, low], axis=0)

    def times_table(field):
        h, l = split(field)
        return jnp.dot(jnp.concatenate([h, l, h], axis=1), table_right, preferred_element_type=F32)

    def table_times(field):
        h, l = split(field)
        return jnp.dot(table_left, jnp.concatenate([h, l, h], axis=0), preferred_element_type=F32)

    pl.semaphore_wait(barrier, len(greeted))

    def copy(src, dst, send, recv, target):
        return pltpu.make_async_remote_copy(
            src_ref=src, dst_ref=dst, send_sem=send, recv_sem=recv, device_id=target, device_id_type=MESH
        )

    def rows(start, count):
        return pl.ds(pl.multiple_of(start, 8), count)

    def wait_rows(sem, count):
        ref = orb_ref.at[0, pl.ds(0, count)]
        pltpu.make_async_copy(ref, ref, sem).wait()

    piece = size // RING_X
    part = piece // Z_LO
    twin = (device(x * CORES + 1 - core, z_lo), plane)
    own_rows = rows(x * piece, piece)

    def core_copy(s):
        return copy(cand.at[s, :, 1 - core], crossed.at[s], core_send.at[s], core_recv.at[s], twin)

    def mix(s):
        core_copy(s).wait_recv()
        mixed[s] = cand[s, :, core] + crossed[s]

    def spread_out(i):
        s, j0, nj = phi_parts[i]
        js = pl.ds(j0, nj)
        for k in range(1, RING_X):
            to = lax.rem(x + k, RING_X)
            copy(
                mixed.at[s, js, rows(to * piece, piece)], spread.at[s, js, x],
                spread_send.at[i], spread_recv.at[i], (device(to * CORES + core, z_lo), plane),
            ).start()
        spread[s, js, x] = mixed[s, js, own_rows]

    def reduce_z(i):
        s, j0, nj = phi_parts[i]
        js = pl.ds(j0, nj)
        wait_rows(spread_recv.at[i], (RING_X - 1) * nj * piece)
        total = spread[s, js, 0]
        for k in range(1, RING_X):
            total = total + spread[s, js, k]
        reduced[s, js] = total
        for z in levels:
            copy(
                reduced.at[s, js, rows(z * part, part)], summed.at[s, js, z_lo],
                z_send.at[i], z_recv.at[i], (device(here, z), plane),
            ).start()
        summed[s, js, z_lo] = reduced[s, js, rows(z_lo * part, part)]

    def gather_z(i):
        s, j0, nj = phi_parts[i]
        js = pl.ds(j0, nj)
        wait_rows(z_recv.at[i], (Z_LO - 1) * nj * part)
        total = summed[s, js, 0]
        for k in range(1, Z_LO):
            total = total + summed[s, js, k]
        finest = rows(x * piece + z_lo * part, part)
        phi[s, js, core, finest] = total
        for z in levels:
            where = phi.at[s, js, core, finest]
            copy(where, where, up_send.at[i], up_recv.at[i], (device(here, z), plane)).start()

    def gather_x(i):
        s, j0, nj = phi_parts[i]
        js = pl.ds(j0, nj)
        wait_rows(up_recv.at[i], (Z_LO - 1) * nj * part)
        if i == len(phi_parts) - 1:
            for target in column:
                pl.semaphore_signal(calm, inc=1, device_id=target, device_id_type=MESH)
        for k in range(1, RING_X):
            where = phi.at[s, js, core, own_rows]
            to = (device(lax.rem(x + k, RING_X) * CORES + core, z_lo), plane)
            copy(where, where, gath_send.at[i], gath_recv.at[i], to).start()

    def half_copy(i):
        s, j0, nj = phi_parts[i]
        where = phi.at[s, pl.ds(j0, nj), core]
        return copy(where, where, half_send.at[i], half_recv.at[i], twin)

    def gather_core(i):
        wait_rows(gath_recv.at[i], (RING_X - 1) * phi_parts[i][2] * piece)
        half_copy(i).start()

    def all_calm():
        pl.semaphore_wait(calm, len(column))

    def have_phi(i):
        half_copy(i).wait_recv()

    def phi_rows(s, x0, nx):
        return phi[s, pl.ds(x0 // CORES, nx // CORES)].reshape(nx * size, size)

    def wait_blocks(sem, count):
        ref = landed.at[0, 0, pl.ds(0, count)]
        pltpu.make_async_copy(ref, ref, sem).wait()

    own = pl.ds(pl.multiple_of(plane * slab, slab), slab)

    def pair(i):
        s, x0, nx, b0, nb = pair_parts[i]
        for b in range(b0, b0 + nb):
            field = orb_ref[b, pl.ds(x0 * size, nx * size)] * phi_rows(s, x0, nx)
            field = times_table(field)
            field = jnp.concatenate([field[j * size : (j + 1) * size] for j in range(nx)], axis=1)
            field = table_times(field)
            for j in range(nx):
                sent[s, b, x0 + j] = field[:, j * size : (j + 1) * size]
        for b in range(b0, b0 + nb):
            landed[s, b, pl.ds(plane * slab + x0, nx)] = sent[s, b, pl.ds(x0, nx), own]

    def send_pair(i, targets):
        s, x0, nx, b0, nb = pair_parts[i]
        for q in targets:
            copy(
                sent.at[s, pl.ds(b0, nb), pl.ds(x0, nx), pl.ds(pl.multiple_of(q * slab, slab), slab)],
                landed.at[s, pl.ds(b0, nb), pl.ds(plane * slab + x0, nx)],
                fwd_send.at[i], fwd_recv.at[i], (band, q),
            ).start()

    arrived = set()

    def middle(s, b):
        for i, (s1, _, nx, b0, nb) in enumerate(pair_parts):
            if s1 == s and b0 <= b < b0 + nb and i not in arrived:
                arrived.add(i)
                wait_blocks(fwd_recv.at[i], (planes - 1) * nx * nb)
        source = landed.at[s, b].reshape(size * slab, size)
        target = filtered.at[s, b].reshape(size * slab, size)
        field = jnp.concatenate([source[pl.ds(k, size, stride=slab), :] for k in range(slab)], axis=1)
        field = table_times(field) * filt[...]
        field = table_times(field)
        for k in range(slab):
            target[pl.ds(k, size, stride=slab), :] = field[:, k * size : (k + 1) * size]
        for q in partners:
            copy(
                filtered.at[s, b, pl.ds(pl.multiple_of(q * slab, slab), slab)], returned.at[s, b, :, own],
                back_send.at[s, b], back_recv.at[s, b], (band, q),
            ).start()
        returned[s, b, :, own] = filtered[s, b, own]

    def last(s, b):
        wait_blocks(back_recv.at[s, b], (planes - 1) * slab)
        field = table_times(jnp.concatenate([returned[s, b, j] for j in range(slab)], axis=1))
        field = jnp.concatenate([field[:, j * size : (j + 1) * size] for j in range(slab)], axis=0)
        field = times_table(field) * phi_rows(s, 0, slab)
        out_ref[b] = field if s == 0 else out_ref[b] + field

    def screen():
        loads[3].wait()
        row = lax.broadcasted_iota(jnp.int32, (size, size), 0)
        col = lax.broadcasted_iota(jnp.int32, (size, size), 1)

        def wave(index, cell):
            return jnp.where(index < size // 2, index, index - size).astype(F32) * (2.0 * math.pi / cell)

        wave_ac = wave(row, 41.04) ** 2 + wave(col, 20.52) ** 2
        for k in range(slab):
            wave_b = wave(jnp.full((size, size), plane * slab + k, jnp.int32), 41.04)
            squared = wave_ac + wave_b * wave_b
            safe = jnp.where(squared > 0, squared, 1.0)
            screened = -4.0 * math.pi * (1.0 - jnp.exp(-safe / (4.0 * OMEGA * OMEGA))) / safe
            screened = jnp.where(squared > 0, screened, -math.pi / (OMEGA * OMEGA))
            keep = mask_ref[pl.ds(k, size, stride=slab), :].astype(F32)
            filt[:, k * size : (k + 1) * size] = screened * keep * (1.0 / (size * size * size))

    for s in range(steps):
        core_copy(s).start()
    mix(0)
    spread_out(0)
    mix(1)
    spread_out(1)
    screen()
    reduce_z(0)
    gather_z(0)
    reduce_z(1)
    gather_x(0)
    gather_z(1)
    gather_core(0)
    gather_x(1)
    have_phi(0)
    pair(0)
    all_calm()
    send_pair(0, partners)
    pair(1)
    send_pair(1, partners)
    gather_core(1)
    have_phi(1)
    pair(2)
    send_pair(2, partners)
    pair(3)
    send_pair(3, partners)
    units = [(s, b) for s in range(steps) for b in range(bands)]
    for unit in units:
        middle(*unit)
    for s in range(steps):
        core_copy(s).wait_send()
    for i, (_, _, nj) in enumerate(phi_parts):
        wait_rows(spread_send.at[i], (RING_X - 1) * nj * piece)
        wait_rows(z_send.at[i], (Z_LO - 1) * nj * part)
        wait_rows(up_send.at[i], (Z_LO - 1) * nj * part)
        wait_rows(gath_send.at[i], (RING_X - 1) * nj * piece)
        half_copy(i).wait_send()
    for i, (_, _, nx, _, nb) in enumerate(pair_parts):
        wait_blocks(fwd_send.at[i], (planes - 1) * nx * nb)
    for unit in units:
        last(*unit)
    for unit in units:
        wait_blocks(back_send.at[unit], (planes - 1) * slab)


def body(planes, orbitals, plan, cutoff_mask):
    bands, slab, size = orbitals.shape[:3]
    steps = plan.shape[0]
    phi_parts = [(0, 0, 4), (1, 0, 4)]
    pair_parts = [(0, 0, 8, 0, 1), (0, 0, 8, 1, 1), (1, 0, 8, 0, 1), (1, 0, 8, 1, 1)]
    hbm = pl.BlockSpec(memory_space=pltpu.HBM)
    vmem = pltpu.VMEM
    dma = pltpu.SemaphoreType.DMA
    unit = (steps, bands)
    planes_per_core = slab // CORES
    parts, pairs = len(phi_parts), len(pair_parts)
    out = pl.pallas_call(
        functools.partial(kernel, planes, steps, bands, size, slab, phi_parts, pair_parts),
        out_shape=jax.ShapeDtypeStruct((bands, slab * size, size), F32),
        in_specs=[hbm, hbm, hbm, hbm],
        out_specs=pl.BlockSpec(memory_space=vmem),
        scratch_shapes=[
            pltpu.SMEM((steps,), jnp.int32),
            vmem((bands, slab * size, size), F32),
            vmem((size * slab, size), jnp.int32),
            vmem((size, size), F32),
            vmem((size, slab * size), F32),
            vmem((steps, planes_per_core, CORES, size, size), F32),
            vmem((steps, planes_per_core, size, size), F32),
            vmem((steps, planes_per_core, size, size), F32),
            vmem((steps, planes_per_core, RING_X, size // RING_X, size), F32),
            vmem((steps, planes_per_core, size // RING_X, size), F32),
            vmem((steps, planes_per_core, Z_LO, size // RING_X // Z_LO, size), F32),
            vmem((steps, planes_per_core, CORES, size, size), F32),
            vmem(unit + (slab, size, size), F32),
            vmem(unit + (size, slab, size), F32),
            vmem(unit + (size, slab, size), F32),
            vmem(unit + (slab, size, size), F32),
            pltpu.SemaphoreType.REGULAR,
            dma((4,)), dma((steps,)), dma((steps,)),
            *(dma((parts,)) for _ in range(10)),
            dma((pairs,)), dma((pairs,)),
            dma(unit), dma(unit),
        ],
        compiler_params=pltpu.CompilerParams(
            collective_id=0, has_side_effects=True, vmem_limit_bytes=40 * 2**20
        ),
    )(
        *(
            pltpu.with_memory_space_constraint(value, pltpu.HBM)
            for value in (
                plan,
                orbitals.reshape(bands, slab * size, size),
                cutoff_mask.reshape(size * slab, size),
                jnp.asarray(cas_table(size)),
            )
        )
    )
    return out.reshape(orbitals.shape)


def solution(mesh):
    return jax.shard_map(
        functools.partial(body, mesh.shape["plane"]),
        mesh=mesh,
        in_specs=(P("band", "plane", None, None), P(), P(None, "plane", None)),
        out_specs=P("band", "plane", None, None),
        check_vma=False,
    )
```

time: 489 us -> 135 us (0.28)
  waiting for transfers between devices: 405 us -> 0 us
  Pallas kernels: 0 us -> 133 us
  starting transfers between devices: 35.6 us -> 0 us
  between operations: 18.5 us -> 0.01 us
  matrix products: 17.4 us -> 0 us
  local copies, waits for them, and re-layouts: 8.41 us -> 0.97 us
    psum x1 -> x0, waiting for transfers between devices: 277 us -> none  [broadcast(): return lax.psum(kept, axis)]
    pallas_call x0 -> x1, Pallas kernels: none -> 133 us  [body(): pl.pallas_call(functools.partial(kernel, planes, steps, bands, size, slab...]
    all_to_all x4 -> x0, waiting for transfers between devices: 129 us -> none  [the longest x2 66.3 us: filter_split(): lax.all_to_all(back, 'plane', split_axis=1, concat_axis=2, tiled=True)]
    all_to_all x4 -> x0, starting transfers between devices: 35.6 us -> none  [the longest x2 19.6 us: body(): lax.all_to_all(near, 'plane', split_axis=2, concat_axis=1, tiled=True)]
    dot_general x12 -> x0, matrix products: 17.4 us -> none  [the longest x4 6.99 us: along_last(): jnp.einsum('bxyz,kz->bxyk', field, table, precision=lax.Precision.HIGHEST)]
    transpose x4 -> x0, local copies, waits for them, and re-layouts: 6.37 us -> none  [the longest x2 3.18 us: along_first(): jnp.einsum('bxyz,kx->bkyz', field, table, precision=lax.Precision.HIGHEST)]
  transfers between devices with their start and end apart: 5 -> 0, of which waited for: 5 -> 0; matrix products, arithmetic and copies ran while one was open for 3% -> 0% of each run, Pallas kernels for 0% -> 0%
where the time goes in v2:
time: 135 us; the launch traced here: 134 us
  Pallas kernels  133 us (99%)
    pallas_call x1, Pallas kernels, body(): pl.pallas_call(functools.partial(kernel, planes, steps, bands, size, slab...  133 us

profile of v2, /device:TPU:6, one launch (start us, length us, event | category | flops | bytes accessed | tf_op | source)
XLA Modules:
  0.0 133.8 jit_solution(2168293017701777744)
XLA Ops:
  0.0 132.8 %shard_map.46 = f32[2,1024,128]{2,1,0:T(8,128)S(1)} custom-call(s32[2]{0:T(128)} %plan_hbm.1, f32[2,1024,128]{2,1,0:T(8,128)} %bitcast.4, s32[1024,128]{1,0:T(8,128)} %bitcast.5, f32[128,128]{1,0:T(8,128)} %constant.2.clone.table_hbm), custom_call_target="tpu_custom_call" | custom-call | tf_op jit(solution)/shard_map/pallas_call | solution.py:323
  132.8 1.0 copy.6

commit v3 on v2

--- a/solution.py
+++ b/solution.py
@@ -54,6 +54,15 @@
     partners = [lax.rem(y + far, rings) * 2 + lax.rem(z_hi + other, 2) for far, other in order]
     levels = [lax.rem(z_lo + k, Z_LO) for k in range(1, Z_LO)]
 
+    loads = [
+        pltpu.make_async_copy(source, target, in_sem.at[i])
+        for i, (source, target) in enumerate(
+            ((plan_hbm, plan_ref), (orb_hbm, orb_ref), (table_hbm, table_ref), (mask_hbm, mask_ref))
+        )
+    ]
+    for load in loads:
+        load.start()
+
     barrier = pltpu.get_barrier_semaphore()
     greeted = [(device(lax.rem(x + k, RING_X) * CORES + core, z_lo), plane) for k in range(1, RING_X)]
     greeted += [(device(x * CORES + 1 - core, z_lo), plane)]
@@ -68,34 +77,27 @@
     for target in greeted:
         pl.semaphore_signal(barrier, inc=1, device_id=target, device_id_type=MESH)
 
-    loads = [
-        pltpu.make_async_copy(source, target, in_sem.at[i])
-        for i, (source, target) in enumerate(
-            ((plan_hbm, plan_ref), (orb_hbm, orb_ref), (table_hbm, table_ref), (mask_hbm, mask_ref))
-        )
-    ]
-    for load in loads:
-        load.start()
     loads[0].wait()
     loads[1].wait()
-    for s in range(steps):
+    def times_table(field):
+        high, low = split(table_ref[...])
+        table_right = jnp.concatenate([high, high, low], axis=0)
+        h, l = split(field)
+        return jnp.dot(jnp.concatenate([h, l, h], axis=1), table_right, preferred_element_type=F32)
+
+    def table_times(field):
+        high, low = split(table_ref[...])
+        table_left = jnp.concatenate([high, high, low], axis=1)
+        h, l = split(field)
+        return jnp.dot(table_left, jnp.concatenate([h, l, h], axis=0), preferred_element_type=F32)
+
+    def candidate(s):
         first = (plan_ref[s] == 2 * band).astype(F32)
         second = (plan_ref[s] == 2 * band + 1).astype(F32)
         chosen = orb_ref[0] * first + orb_ref[1] * second
         cand[s] = chosen.reshape(cand.shape[1:])
-    loads[2].wait()
-    high, low = split(table_ref[...])
-    table_left = jnp.concatenate([high, high, low], axis=1)
-    table_right = jnp.concatenate([high, high, low], axis=0)
-
-    def times_table(field):
-        h, l = split(field)
-        return jnp.dot(jnp.concatenate([h, l, h], axis=1), table_right, preferred_element_type=F32)
-
-    def table_times(field):
-        h, l = split(field)
-        return jnp.dot(table_left, jnp.concatenate([h, l, h], axis=0), preferred_element_type=F32)
-
+
+    candidate(0)
     pl.semaphore_wait(barrier, len(greeted))
 
     def copy(src, dst, send, recv, target):
@@ -232,7 +234,8 @@
         field = table_times(field)
         for k in range(slab):
             target[pl.ds(k, size, stride=slab), :] = field[:, k * size : (k + 1) * size]
-        for q in partners:
+        r = (0, 3, 7, 11)[s * bands + b]
+        for q in partners[r:] + partners[:r]:
             copy(
                 filtered.at[s, b, pl.ds(pl.multiple_of(q * slab, slab), slab)], returned.at[s, b, :, own],
                 back_send.at[s, b], back_recv.at[s, b], (band, q),
@@ -247,6 +250,7 @@
         out_ref[b] = field if s == 0 else out_ref[b] + field
 
     def screen():
+        loads[2].wait()
         loads[3].wait()
         row = lax.broadcasted_iota(jnp.int32, (size, size), 0)
         col = lax.broadcasted_iota(jnp.int32, (size, size), 1)
@@ -264,32 +268,39 @@
             keep = mask_ref[pl.ds(k, size, stride=slab), :].astype(F32)
             filt[:, k * size : (k + 1) * size] = screened * keep * (1.0 / (size * size * size))
 
-    for s in range(steps):
-        core_copy(s).start()
+    core_copy(0).start()
+    candidate(1)
+    core_copy(1).start()
     mix(0)
     spread_out(0)
+    spread_out(1)
     mix(1)
-    spread_out(1)
+    spread_out(2)
     screen()
     reduce_z(0)
+    reduce_z(1)
+    reduce_z(2)
     gather_z(0)
-    reduce_z(1)
+    gather_z(1)
+    gather_z(2)
     gather_x(0)
-    gather_z(1)
+    gather_x(1)
+    gather_x(2)
     gather_core(0)
-    gather_x(1)
+    gather_core(1)
     have_phi(0)
+    have_phi(1)
     pair(0)
     all_calm()
     send_pair(0, partners)
     pair(1)
-    send_pair(1, partners)
-    gather_core(1)
-    have_phi(1)
+    send_pair(1, partners[3:] + partners[:3])
+    gather_core(2)
+    have_phi(2)
     pair(2)
-    send_pair(2, partners)
+    send_pair(2, partners[7:] + partners[:7])
     pair(3)
-    send_pair(3, partners)
+    send_pair(3, partners[11:] + partners[:11])
     units = [(s, b) for s in range(steps) for b in range(bands)]
     for unit in units:
         middle(*unit)
@@ -312,7 +323,7 @@
 def body(planes, orbitals, plan, cutoff_mask):
     bands, slab, size = orbitals.shape[:3]
     steps = plan.shape[0]
-    phi_parts = [(0, 0, 4), (1, 0, 4)]
+    phi_parts = [(0, 0, 2), (0, 2, 2), (1, 0, 4)]
     pair_parts = [(0, 0, 8, 0, 1), (0, 0, 8, 1, 1), (1, 0, 8, 0, 1), (1, 0, 8, 1, 1)]
     hbm = pl.BlockSpec(memory_space=pltpu.HBM)
     vmem = pltpu.VMEM

time: 135 us -> 134 us (level)
  Pallas kernels: 133 us -> 131 us
    pallas_call x1, Pallas kernels: 133 us -> 131 us  [body(): pl.pallas_call(functools.partial(kernel, planes, steps, bands, size, slab...]
where the time goes in v3:
time: 134 us; the launch traced here: 132 us
  Pallas kernels  131 us (98%)
    pallas_call x1, Pallas kernels, body(): pl.pallas_call(functools.partial(kernel, planes, steps, bands, size, slab...  131 us

profile of v3, /device:TPU:6, one launch (start us, length us, event | category | flops | bytes accessed | tf_op | source)
XLA Modules:
  0.0 131.8 jit_solution(814610662572142357)
XLA Ops:
  0.0 130.8 %shard_map.46 = f32[2,1024,128]{2,1,0:T(8,128)S(1)} custom-call(s32[2]{0:T(128)} %plan_hbm.1, f32[2,1024,128]{2,1,0:T(8,128)} %bitcast.4, s32[1024,128]{1,0:T(8,128)} %bitcast.5, f32[128,128]{1,0:T(8,128)} %constant.2.clone.table_hbm), custom_call_target="tpu_custom_call" | custom-call | tf_op jit(solution)/shard_map/pallas_call | solution.py:334
  130.8 1.0 copy.6

commit v4 on v3

--- a/solution.py
+++ b/solution.py
@@ -24,8 +24,16 @@
 
 def split(value):
     high = value.astype(BF16)
-    low = (value - high.astype(F32)).astype(BF16)
-    return high, low
+    rest = value - high.astype(F32)
+    middle = rest.astype(BF16)
+    return high, middle, (rest - middle.astype(F32)).astype(BF16)
+
+
+def terms(value, first, exact):
+    h, m, l = split(value)
+    if not exact:
+        return (h, h, m) if first else (h, m, h)
+    return (h, h, m, m, h, l) if first else (h, m, h, m, l, h)
 
 
 def kernel(
@@ -79,17 +87,15 @@
 
     loads[0].wait()
     loads[1].wait()
-    def times_table(field):
-        high, low = split(table_ref[...])
-        table_right = jnp.concatenate([high, high, low], axis=0)
-        h, l = split(field)
-        return jnp.dot(jnp.concatenate([h, l, h], axis=1), table_right, preferred_element_type=F32)
-
-    def table_times(field):
-        high, low = split(table_ref[...])
-        table_left = jnp.concatenate([high, high, low], axis=1)
-        h, l = split(field)
-        return jnp.dot(table_left, jnp.concatenate([h, l, h], axis=0), preferred_element_type=F32)
+    def times_table(field, exact=False):
+        left = jnp.concatenate(terms(field, False, exact), axis=1)
+        right = jnp.concatenate(terms(table_ref[...], True, exact), axis=0)
+        return jnp.dot(left, right, preferred_element_type=F32)
+
+    def table_times(field, exact=False):
+        left = jnp.concatenate(terms(table_ref[...], True, exact), axis=1)
+        right = jnp.concatenate(terms(field, False, exact), axis=0)
+        return jnp.dot(left, right, preferred_element_type=F32)
 
     def candidate(s):
         first = (plan_ref[s] == 2 * band).astype(F32)
@@ -203,9 +209,9 @@
         s, x0, nx, b0, nb = pair_parts[i]
         for b in range(b0, b0 + nb):
             field = orb_ref[b, pl.ds(x0 * size, nx * size)] * phi_rows(s, x0, nx)
-            field = times_table(field)
+            field = times_table(field, exact=True)
             field = jnp.concatenate([field[j * size : (j + 1) * size] for j in range(nx)], axis=1)
-            field = table_times(field)
+            field = table_times(field, exact=True)
             for j in range(nx):
                 sent[s, b, x0 + j] = field[:, j * size : (j + 1) * size]
         for b in range(b0, b0 + nb):
@@ -230,7 +236,7 @@
         source = landed.at[s, b].reshape(size * slab, size)
         target = filtered.at[s, b].reshape(size * slab, size)
         field = jnp.concatenate([source[pl.ds(k, size, stride=slab), :] for k in range(slab)], axis=1)
-        field = table_times(field) * filt[...]
+        field = table_times(field, exact=True) * filt[...]
         field = table_times(field)
         for k in range(slab):
             target[pl.ds(k, size, stride=slab), :] = field[:, k * size : (k + 1) * size]

time: 134 us -> 134 us (level)
  no operation moved by 1% of the time
where the time goes in v4:
time: 134 us; the launch traced here: 132 us
  Pallas kernels  131 us (98%)
    pallas_call x1, Pallas kernels, body(): pl.pallas_call(functools.partial(kernel, planes, steps, bands, size, slab...  131 us

profile of v4, /device:TPU:6, one launch (start us, length us, event | category | flops | bytes accessed | tf_op | source)
XLA Modules:
  0.0 132.1 jit_solution(14809644072323656908)
XLA Ops:
  0.0 131.1 %shard_map.46 = f32[2,1024,128]{2,1,0:T(8,128)S(1)} custom-call(s32[2]{0:T(128)} %plan_hbm.1, f32[2,1024,128]{2,1,0:T(8,128)} %bitcast.4, s32[1024,128]{1,0:T(8,128)} %bitcast.5, f32[128,128]{1,0:T(8,128)} %constant.2.clone.table_hbm), custom_call_target="tpu_custom_call" | custom-call | tf_op jit(solution)/shard_map/pallas_call | solution.py:340
  131.1 1.0 copy.6

commit v5 on v4

--- a/solution.py
+++ b/solution.py
@@ -58,8 +58,8 @@
     def device(e, z):
         return (e // CORES) * (CORES * Z_LO) + z * CORES + lax.rem(e, CORES)
 
-    order = [(4, 1), (4, 0), (0, 1), (1, 1), (3, 0), (5, 0), (7, 1), (2, 1), (6, 1), (2, 0), (6, 0), (3, 1), (5, 1), (1, 0), (7, 0)]
-    partners = [lax.rem(y + far, rings) * 2 + lax.rem(z_hi + other, 2) for far, other in order]
+    order = [(4, 1), (4, 0), (0, 1), (1, 1), (3, 0), (7, 1), (5, 0), (2, 1), (2, 0), (6, 1), (6, 0), (3, 1), (1, 0), (5, 1), (7, 0)]
+    partners = [lax.rem(y + far + core * (2 * rings - 2 * far), rings) * 2 + lax.rem(z_hi + other, 2) for far, other in order]
     levels = [lax.rem(z_lo + k, Z_LO) for k in range(1, Z_LO)]
 
     loads = [

time: 134 us -> 134 us (level)
  no operation moved by 1% of the time
where the time goes in v5:
time: 134 us; the launch traced here: 132 us
  Pallas kernels  131 us (98%)
    pallas_call x1, Pallas kernels, body(): pl.pallas_call(functools.partial(kernel, planes, steps, bands, size, slab...  131 us

profile of v5, /device:TPU:6, one launch (start us, length us, event | category | flops | bytes accessed | tf_op | source)
XLA Modules:
  0.0 131.8 jit_solution(6131982795659971413)
XLA Ops:
  0.0 130.8 %shard_map.46 = f32[2,1024,128]{2,1,0:T(8,128)S(1)} custom-call(s32[2]{0:T(128)} %plan_hbm.1, f32[2,1024,128]{2,1,0:T(8,128)} %bitcast.4, s32[1024,128]{1,0:T(8,128)} %bitcast.5, f32[128,128]{1,0:T(8,128)} %constant.2.clone.table_hbm), custom_call_target="tpu_custom_call" | custom-call | tf_op jit(solution)/shard_map/pallas_call | solution.py:340
  130.8 1.0 copy.6
